TPU v7x, 32 devices: a whole 2x2x4 slice. The times are simulated.
32 devices in a mesh: parts: 1, ctx: 4 (over z), pb: 4 (over y, x), row: 2 (over core).
Axes of the slice: x: 2, y: 2, z: 4, core: 2. Of those that a mesh axis runs over, the one named last changes fastest.
Arguments:
- queries: bfloat16 [2048, 3072], P(('parts', 'ctx', 'pb', 'row')), may hold values from -10 to 10
- cache_keys: bfloat16 [4096, 192], P(('parts', 'ctx')), may hold values from -10 to 10
- cache_values: bfloat16 [4096, 128], P(('parts', 'ctx')), may hold values from -6 to 6
- span_keys: bfloat16 [2048, 192], P(('parts', 'ctx')), may hold values from -10 to 10
- span_values: bfloat16 [2048, 128], P(('parts', 'ctx')), may hold values from -6 to 6
- pool_keys: float32 [32, 192], replicated, may hold values from 0.2 to 0.6
- pool_values: float32 [32, 128], replicated, may hold values from 0.05 to 0.3
- gate_logits: bfloat16 [2048, 48], P(('parts', 'ctx', 'pb', 'row')), may hold values from -6 to 6
- chosen_blocks: int32 [32, 16], P(('parts', 'ctx', 'pb', 'row')), may hold values from 0 to 95, as said below
- valid_counts: int32 [32], P(('parts', 'ctx', 'pb', 'row')), may hold values from 4 to 16
Outputs:
- mixed: bfloat16 [2048, 2048], P(('parts', 'ctx', 'pb', 'row'))
Inputs may be any that keep to these rules, and one draw needn't show every extreme that they name: `chosen_blocks`: slot 0 of tile t holds the tile's own block 64 + t. Slot s > 0 holds a block of the cache stored by ctx index (c + s) mod (4), where c is the ctx index that holds tile t; the blocks of one tile are distinct. Slots at or beyond the tile's valid count hold blocks too and are ignored.
All inputs are finite; a program needn't handle non-finite values.
Results may differ from a plain program's by a relative error of at most 0.0034.
The roundings to bfloat16 on the way count: a program that leaves them out, or rounds other values in their place, can miss the bound.
Values may be sent and summed in bfloat16 or wider, within the bound.
A program may use at most 64 MiB of HBM per device.

v0:
```python
import math

import jax
import jax.numpy as jnp
from jax import lax
from jax.sharding import PartitionSpec as P

HEADS = 16
CLEN = 32
STRIDE = 16
BLOCK = 64
WINDOW = 256


NEG_FILL = -1e30


def from_behind(value, axis, steps):
    count = lax.axis_size(axis)
    pairs = [(source, (source + steps) % count) for source in range(count)]
    return lax.ppermute(value, axis, pairs)


def pool_blocks(rows, extra, weights, stride):
    joined = jnp.concatenate([rows, extra], axis=0).astype(jnp.float32)
    blocks = rows.shape[0] // stride
    grouped = joined.reshape(blocks + 1, stride, rows.shape[1])
    leading = jnp.sum(grouped[:-1] * weights[None, :stride, :], axis=1)
    trailing = jnp.sum(grouped[1:] * weights[None, stride:, :], axis=1)
    return (leading + trailing).astype(jnp.bfloat16)


def attend(query_rows, keys, values, visible, score_scale):
    scores = jnp.dot(query_rows, keys.T, preferred_element_type=jnp.float32) * score_scale
    scores = jnp.where(visible, scores, NEG_FILL)
    highest = jnp.max(scores, axis=1, keepdims=True)
    exponent = jnp.where(visible, jnp.exp(scores - highest), 0.0)
    weights = exponent.astype(jnp.bfloat16)
    numerator = jnp.dot(weights, values, preferred_element_type=jnp.float32)
    return numerator / jnp.sum(exponent, axis=1, keepdims=True)


def local(
    queries,
    cache_keys,
    cache_values,
    span_keys,
    span_values,
    pool_keys,
    pool_values,
    gate_logits,
    chosen_blocks,
    valid_counts,
):
    owners = lax.axis_size("ctx")
    ctx_place = lax.axis_index("ctx")
    tile_place = lax.axis_index("pb") * lax.axis_size("row") + lax.axis_index("row")
    cache_len, key_width = cache_keys.shape
    value_width = cache_values.shape[1]
    span_len = span_keys.shape[0]
    tokens = queries.shape[0]
    tiles_here = chosen_blocks.shape[0]
    score_scale = 1.0 / math.sqrt(key_width)
    context_start = cache_len * owners
    local_start = tile_place * tokens
    first_pos = context_start + ctx_place * span_len + local_start
    row_count = tokens * HEADS
    query_rows = queries.reshape(row_count, key_width)
    row_pos = first_pos + jnp.arange(row_count, dtype=jnp.int32) // HEADS
    leader = ctx_place == 0
    outgoing = (
        jnp.where(leader, span_keys[:STRIDE], cache_keys[:STRIDE]),
        jnp.where(leader, span_values[:STRIDE], cache_values[:STRIDE]),
        span_keys[:STRIDE],
        span_values[:STRIDE],
    )
    heads_next = from_behind((outgoing[0], outgoing[1], outgoing[2], outgoing[3]), "ctx", -1)
    summary_keys = jnp.concatenate(
        [
            pool_blocks(cache_keys, heads_next[0], pool_keys, STRIDE),
            pool_blocks(span_keys, heads_next[2], pool_keys, STRIDE),
        ],
        axis=0,
    )
    summary_values = jnp.concatenate(
        [
            pool_blocks(cache_values, heads_next[1], pool_values, STRIDE),
            pool_blocks(span_values, heads_next[3], pool_values, STRIDE),
        ],
        axis=0,
    )
    cache_blocks = cache_len // STRIDE
    span_blocks = span_len // STRIDE
    per_ctx = cache_blocks + span_blocks
    first_row = jnp.int32(0)
    running_max = jnp.full((row_count,), NEG_FILL, jnp.float32)
    running_sum = jnp.zeros((row_count,), jnp.float32)
    running_out = jnp.zeros((row_count, value_width), jnp.float32)
    part_keys = lax.all_gather(summary_keys, "ctx", axis=0, tiled=True)
    part_values = lax.all_gather(summary_values, "ctx", axis=0, tiled=True)
    length = part_keys.shape[0]
    for lower_row in range(0, length, 512):
        upper_row = min(lower_row + 512, length)
        block_index = first_row + lower_row + jnp.arange(upper_row - lower_row, dtype=jnp.int32)
        owner_of = block_index // per_ctx
        within = block_index % per_ctx
        block_id = jnp.where(
            within < cache_blocks,
            owner_of * cache_blocks + within,
            owners * cache_blocks + owner_of * span_blocks + within - cache_blocks,
        )
        visible = (block_id * STRIDE + CLEN)[None, :] <= row_pos[:, None] + 1
        scores = (
            jnp.dot(
                query_rows, part_keys[lower_row:upper_row].T, preferred_element_type=jnp.float32
            )
            * score_scale
        )
        scores = jnp.where(visible, scores, NEG_FILL)
        new_max = jnp.maximum(running_max, jnp.max(scores, axis=1))
        exponent = jnp.where(visible, jnp.exp(scores - new_max[:, None]), 0.0)
        fading = jnp.exp(running_max - new_max)
        running_sum = running_sum * fading + jnp.sum(exponent, axis=1)
        running_out = running_out * fading[:, None] + jnp.dot(
            exponent.astype(jnp.bfloat16),
            part_values[lower_row:upper_row],
            preferred_element_type=jnp.float32,
        )
        running_max = new_max
    summary_out = running_out / running_sum[:, None]
    reach = chosen_blocks.shape[1] // owners
    arranged = chosen_blocks.reshape(tiles_here, reach, owners)
    column_of = (jnp.arange(owners, dtype=jnp.int32) - ctx_place) % owners
    requested = jnp.take(arranged, column_of, axis=2)
    wanted = lax.all_to_all(requested, "ctx", split_axis=2, concat_axis=2, tiled=True)
    cache_count = cache_len // BLOCK
    span_count = span_len // BLOCK
    from_cache = (wanted < owners * cache_count)[..., None, None]
    cache_slot = jnp.clip(wanted - ctx_place * cache_count, 0, cache_count - 1)
    span_slot = jnp.clip(wanted - owners * cache_count - ctx_place * span_count, 0, span_count - 1)
    served_keys = jnp.where(
        from_cache,
        cache_keys.reshape(cache_count, BLOCK, key_width)[cache_slot],
        span_keys.reshape(span_count, BLOCK, key_width)[span_slot],
    )
    served_values = jnp.where(
        from_cache,
        cache_values.reshape(cache_count, BLOCK, value_width)[cache_slot],
        span_values.reshape(span_count, BLOCK, value_width)[span_slot],
    )
    fetched_keys, fetched_values = (
        lax.all_to_all(served_keys, "ctx", split_axis=2, concat_axis=2, tiled=True),
        lax.all_to_all(served_values, "ctx", split_axis=2, concat_axis=2, tiled=True),
    )
    last_ctx = ctx_place == owners - 1
    tail_rows = from_behind(
        (
            jnp.where(last_ctx, cache_keys[-WINDOW:], span_keys[-WINDOW:]),
            jnp.where(last_ctx, cache_values[-WINDOW:], span_values[-WINDOW:]),
        ),
        "ctx",
        1,
    )
    reach_keys = jnp.concatenate([tail_rows[0], span_keys], axis=0)
    reach_values = jnp.concatenate([tail_rows[1], span_values], axis=0)
    gate_values = jax.nn.sigmoid(gate_logits.astype(jnp.float32)).reshape(tokens, 3, HEADS)
    offsets = jnp.arange(BLOCK, dtype=jnp.int32)
    near_offsets = jnp.arange(WINDOW + BLOCK, dtype=jnp.int32)
    slot_number = jnp.arange(reach, dtype=jnp.int32)[:, None] * owners + column_of[None, :]
    key_pos = (requested[0][:, :, None] * BLOCK + offsets).reshape(-1)
    usable = jnp.repeat((slot_number < valid_counts[0]).reshape(-1), BLOCK)
    sel_visible = usable[None, :] & (key_pos[None, :] <= row_pos[:, None])
    picked = attend(
        query_rows,
        fetched_keys[0].reshape(-1, key_width),
        fetched_values[0].reshape(-1, value_width),
        sel_visible,
        score_scale,
    )
    begin = local_start + 0
    near_keys = lax.dynamic_slice_in_dim(reach_keys, begin, WINDOW + BLOCK, 0)
    near_values = lax.dynamic_slice_in_dim(reach_values, begin, WINDOW + BLOCK, 0)
    near_pos = context_start + ctx_place * span_len - WINDOW + begin + near_offsets
    near_visible = (near_pos[None, :] <= row_pos[:, None]) & (
        near_pos[None, :] > row_pos[:, None] - WINDOW
    )
    nearby = attend(query_rows, near_keys, near_values, near_visible, score_scale)
    mixed = (
        gate_values[:, 0, :, None] * summary_out.reshape(BLOCK, HEADS, value_width)
        + gate_values[:, 1, :, None] * picked.reshape(BLOCK, HEADS, value_width)
        + gate_values[:, 2, :, None] * nearby.reshape(BLOCK, HEADS, value_width)
    )
    outputs = mixed.reshape(BLOCK, HEADS * value_width).astype(jnp.bfloat16)
    return outputs


def solution(mesh):
    return jax.shard_map(
        local,
        mesh=mesh,
        in_specs=(
            P(("parts", "ctx", "pb", "row"), None),
            P(("parts", "ctx"), None),
            P(("parts", "ctx"), None),
            P(("parts", "ctx"), None),
            P(("parts", "ctx"), None),
            P(),
            P(),
            P(("parts", "ctx", "pb", "row"), None),
            P(("parts", "ctx", "pb", "row"), None),
            P(("parts", "ctx", "pb", "row")),
        ),
        out_specs=P(("parts", "ctx", "pb", "row"), None),
        check_vma=False,
    )
```

profile of v0, /device:TPU:0, one launch (start us, length us, event | category | flops | bytes accessed | tf_op | source)
XLA Modules:
  0.0 91.8 jit_solution(5316688061465802636)
XLA Ops:
  0.0 1.3 %copy.79 = bf16[1024,192]{1,0:T(8,128)(2,1)S(1)} copy(bf16[1024,192]{0,1:T(8,128)(2,1)} %param.11) | data formatting | bytes 786432 | tf_op args[1]
  1.3 1.1 %copy.77 = bf16[512,192]{1,0:T(8,128)(2,1)S(1)} copy(bf16[512,192]{0,1:T(8,128)(2,1)} %param.13) | data formatting | bytes 393216 | tf_op args[3]
  2.4 0.6 slice_select_fusion.2
  3.0 5.1 %collective-permute-start = (bf16[16,192]{1,0:T(8,128)(2,1)}, bf16[16,192]{1,0:T(8,128)(2,1)}, u32[]{:S(2)}, u32[]{:S(2)}) collective-permute-start(bf16[16,192]{1,0:T(8,128)(2,1)} %get-tuple-element.13), channel_id=1, source_target_pairs={{0,24},{8,0},{16,8},{24,16},{1,25},{9,1},{17,9},{25,17},{2,26},{10... | collective-permute-start | bytes 18440 | tf_op jit(solution)/shard_map/ppermute | solution.py:21
  8.0 0.4 collective-permute-start.1
  8.5 1.3 %slice_select_fusion.3 = (bf16[16,128]{1,0:T(8,128)(2,1)}, bf16[16,128]{1,0:T(8,128)(2,1)}) fusion(bf16[1024,128]{1,0:T(8,128)(2,1)} %param.12, pred[]{:T(512)S(6)} %eq.10, bf16[512,128]{1,0:T(8,128)(2,1)} %param.14), kind=kLoop, calls=%fused_computation.87 | loop fusion | flops 2048 | bytes 16385 | tf_op jit(solution)/shard_map/jit(_where)/select_n | solution.py:73
  9.8 0.4 collective-permute-start.2
  10.3 0.5 broadcast.494
  10.8 1.3 %reduce.3 = s32[16]{0:T(128)S(1)} reduce(s32[1,16]{1,0:T(1,128)} %param.18, s32[]{:T(128)} %broadcast.494), dimensions={0}, to_apply=%param.18.reduce_sub_computation.3 | reduce | bytes 132 | tf_op args[8]
  12.2 0.1 copy.82
  12.3 0.6 gather_fusion
  12.9 0.1 copy.84
  13.0 0.7 copy.85
  13.7 5.3 %all-to-all-start = ((s32[1,4,4]{1,0,2:T(1,128)}), s32[1,4,4]{1,0,2:T(1,128)S(1)}, u32[]{:S(2)}, u32[]{:S(2)}) async-start(s32[1,4,4]{1,0,2:T(1,128)} %copy.85), calls=%async_computation | async-start | bytes 4096 | tf_op jit(solution)/shard_map/all_to_all | solution.py:135
  18.9 1.0 %slice_select_fusion = bf16[256,192]{0,1:T(8,128)(2,1)S(1)} fusion(bf16[512,192]{0,1:T(8,128)(2,1)} %param.13, bf16[1024,192]{0,1:T(8,128)(2,1)} %param.11, pred[]{:T(512)S(6)} %eq.11), kind=kLoop, calls=%fused_computation.60 | loop fusion | flops 49152 | bytes 294913 | tf_op jit(solution)/shard_map/jit(_where)/select_n | solution.py:158
  19.9 2.1 %collective-permute-start.4 = (bf16[256,192]{0,1:T(8,128)(2,1)S(1)}, bf16[256,192]{0,1:T(8,128)(2,1)}, u32[]{:S(2)}, u32[]{:S(2)}) collective-permute-start(bf16[256,192]{0,1:T(8,128)(2,1)S(1)} %slice_select_fusion), channel_id=1, source_target_pairs={{0,8},{8,16},{16,24},{24,0},{1,9},{9,17},{17,25},{25,1},{2,10},{10... | collective-permute-start | bytes 294920 | tf_op jit(solution)/shard_map/ppermute | solution.py:21
  22.0 0.6 multiply_add_fusion
  22.8 0.6 reshape.297
  23.4 0.1 copy.83
  24.4 0.1 lt.66
  24.5 0.6 and.99
  25.2 0.7 copy.76
  25.9 0.7 copy.81
  26.6 0.7 copy.97
  27.3 0.1 copy.89
  27.5 0.1 copy.91
  27.6 0.1 copy.86
  27.7 0.1 copy.87
  27.9 0.6 gather_fusion.1
  28.4 0.6 gather_fusion.3
  29.1 0.6 gather_fusion.2
  29.6 0.6 gather_fusion.4
  30.2 0.1 broadcast_select_fusion
  30.3 0.7 copy.95
  31.1 3.6 %all-to-all-start.2 = ((bf16[1,4,4,64,128]{4,3,1,0,2:T(8,128)(2,1)}), bf16[1,4,4,64,128]{4,3,1,0,2:T(8,128)(2,1)S(1)}, u32[]{:S(2)}, u32[]{:S(2)}) async-start(bf16[1,4,4,64,128]{4,3,1,0,2:T(8,128)(2,1)} %copy.95), calls=%async_computation.2 | async-start | bytes 524288 | tf_op jit(solution)/shard_map/all_to_all | solution.py:153
  34.7 0.9 copy_select_fusion
  35.6 2.0 %collective-permute-start.5 = (bf16[256,128]{1,0:T(8,128)(2,1)S(1)}, bf16[256,128]{1,0:T(8,128)(2,1)}, u32[]{:S(2)}, u32[]{:S(2)}) collective-permute-start(bf16[256,128]{1,0:T(8,128)(2,1)S(1)} %slice_select_fusion.1), channel_id=1, source_target_pairs={{0,8},{8,16},{16,24},{24,0},{1,9},{9,17},{17,25},{25,1},{2,10},{10... | collective-permute-start | bytes 196616 | tf_op jit(solution)/shard_map/ppermute | solution.py:21
  37.6 0.7 maximum_convert_fusion.2
  38.4 0.7 maximum_convert_fusion.3
  39.2 0.2 multiply_reduce_fusion.2
  39.4 0.1 multiply_reduce_fusion.6
  39.6 13.2 %all_gather.7 = bf16[384,128]{1,0:T(8,128)(2,1)S(1)} all-gather(bf16[96,128]{1,0:T(8,128)(2,1)S(1)} %pad_maximum_fusion.1), channel_id=1, replica_groups=mesh['parts'=1,'ctx'=4,'pb'=4,'row'=2] {'ctx'}, dimensions={0}, use_global_device_ids=true | all-gather | bytes 122880 | tf_op jit(solution)/shard_map/all_gather | solution.py:100
  52.8 0.8 maximum_convert_fusion
  53.6 0.2 fusion.53
  53.8 0.7 maximum_convert_fusion.1
  54.6 0.5 multiply_reduce_fusion
  55.2 0.3 multiply_reduce_fusion.4
  55.5 13.6 %all_gather.6 = bf16[384,192]{1,0:T(8,128)(2,1)S(1)} all-gather(bf16[96,192]{1,0:T(8,128)(2,1)S(1)} %pad_maximum_fusion), channel_id=1, replica_groups=mesh['parts'=1,'ctx'=4,'pb'=4,'row'=2] {'ctx'}, dimensions={0}, use_global_device_ids=true | all-gather | bytes 184320 | tf_op jit(solution)/shard_map/all_gather | solution.py:99
  69.0 0.4 fusion.60
  69.5 0.3 fusion.9
  69.8 0.7 fusion.5
  70.6 3.7 %all-to-all-start.1 = ((bf16[1,4,4,64,192]{4,3,1,0,2:T(8,128)(2,1)}), bf16[1,4,4,64,192]{4,3,1,0,2:T(8,128)(2,1)S(1)}, u32[]{:S(2)}, u32[]{:S(2)}) async-start(bf16[1,4,4,64,192]{4,3,1,0,2:T(8,128)(2,1)} %copy_select_fusion), calls=%async_computation.1 | async-start | bytes 1048576 | tf_op jit(solution)/shard_map/all_to_all | solution.py:152
  74.3 1.7 %fusion.59 = (f32[1024]{0:T(1024)S(1)}, f32[1024,320]{0,1:T(8,128)S(1)}) fusion(bf16[1024,192]{1,0:T(8,128)(2,1)S(1)} %reshape.297, s32[]{:T(128)S(6)} %select_n.211, bf16[256,192]{0,1:T(8,128)(2,1)} %collective-permute-done.4, bf16[512,192]{0,1:T(8,128)(2,1)S(1)} %copy-done.2, s32[1024]{0:T(1024)S(1)} %broadcast_add_fusion, s32[1024]{0:T(1024)S(1)} %fusion.31, ...), kind=kOutput, calls=%fused_computation.137 | convolution fusion | flops 128039936 | bytes 2012420 | tf_op jit(solution)/shard_map/dot_general | solution.py:34
  76.0 0.4 fusion.11
  76.4 1.5 %convolution_divide_fusion = f32[1024,128]{1,0:T(8,128)S(1)} fusion(f32[1024,320]{0,1:T(8,128)S(1)} %get-tuple-element.29, f32[1024]{0:T(1024)S(1)} %get-tuple-element.28, s32[1024]{0:T(1024)S(1)} %broadcast_add_fusion, s32[1024]{0:T(1024)S(1)} %fusion.31, s32[320]{0:T(512)S(1)} %iota_add_fusion.1, f32[1024]{0:T(1024)S(1)} %fusion.11, s32[]{:T(128)S(6)} %select_n.211, ...), kind=kOutput, calls=%fused_computation.21 | convolution fusion | flops 86147072 | bytes 2049284 | tf_op jit(solution)/shard_map/dot_general | solution.py:39
  78.0 6.4 %all-to-all-done.1 = bf16[1,4,4,64,192]{4,3,1,0,2:T(8,128)(2,1)S(1)} async-done(((bf16[1,4,4,64,192]{4,3,1,0,2:T(8,128)(2,1)}), bf16[1,4,4,64,192]{4,3,1,0,2:T(8,128)(2,1)S(1)}, u32[]{:S(2)}, u32[]{:S(2)}) %all-to-all-start.1) | async-done | bytes 393248 | tf_op jit(solution)/shard_map/all_to_all | solution.py:152
  84.4 1.2 %fusion = (f32[1024]{0:T(1024)S(1)}, f32[1024,1024]{1,0:T(8,128)S(1)}) fusion(s32[1024]{0:T(1024)S(1)} %fusion.31, s32[1024]{0:T(1024)S(1)} %add.265, pred[1024]{0:T(1024)(128)(4,1)S(1)} %copy-done.11, bf16[1024,192]{1,0:T(8,128)(2,1)S(1)} %bitcast.97, bf16[1024,192]{1,0:T(8,128)(2,1)S(1)} %reshape.297), kind=kOutput, calls=%fused_computation.8 | convolution fusion | flops 407895040 | bytes 4994048 | tf_op jit(solution)/shard_map/dot_general | solution.py:34
  85.6 1.9 %fusion.52 = f32[1024]{0:T(1024)S(1)} fusion(f32[1024]{0:T(1024)S(1)} %get-tuple-element.30, f32[1024,1024]{1,0:T(8,128)S(1)} %get-tuple-element.31, s32[1024]{0:T(1024)S(1)} %fusion.31, s32[1024]{0:T(1024)S(1)} %add.265, pred[1024]{0:T(1024)(128)(4,1)S(1)} %copy-done.11), kind=kLoop, calls=%fused_computation.130 | loop fusion | flops 7339008 | bytes 4211712 | tf_op jit(solution)/shard_map/reduce_sum | solution.py:40
  87.5 1.8 %fusion.6 = f32[1024,128]{1,0:T(8,128)S(1)} fusion(bf16[1024,128]{1,0:T(8,128)(2,1)S(1)} %bitcast.98, f32[1024]{0:T(1024)S(1)} %fusion.52, f32[1024,1024]{1,0:T(8,128)S(1)} %get-tuple-element.31, f32[1024]{0:T(1024)S(1)} %get-tuple-element.30, s32[1024]{0:T(1024)S(1)} %fusion.31, s32[1024]{0:T(1024)S(1)} %add.265, pred[1024]{0:T(1024)(128)(4,1)S(1)} %copy-done.11), kind=kOutput, calls=%fused_computation.20 | convolution fusion | flops 275906560 | bytes 4998144 | tf_op jit(solution)/shard_map/dot_general | solution.py:39
  89.5 0.2 mul.192
  89.7 0.4 copy-done.5
  90.2 0.2 mul.223
  90.4 0.2 mul.234
  90.6 1.3 %fusion.25 = bf16[64,2048]{1,0:T(8,128)(2,1)} fusion(f32[64,2048]{1,0:T(8,128)S(1)} %reshape.305, f32[8,8,16,128]{3,2,1,0:T(8,128)S(1)} %bitcast.92, f32[64,2048]{1,0:T(8,128)S(1)} %reshape.304, f32[8,8,16,128]{3,2,1,0:T(8,128)S(1)} %bitcast.91, f32[64,2048]{1,0:T(8,128)S(1)} %reshape.298, f32[8,8,16,128]{3,2,1,0:T(8,128)S(1)} %bitcast.90), kind=kLoop, calls=%fused_computation.40 | loop fusion | flops 786432 | bytes 3407872 | tf_op jit(solution)/shard_map/convert_element_type | solution.py:193
  (75 shorter events, 1.4 us)
Async XLA Ops:
  0.0 22.7 %copy-start.1 = (bf16[1024,128]{1,0:T(8,128)(2,1)S(1)}, bf16[1024,128]{1,0:T(8,128)(2,1)}, u32[]{:S(2)}) copy-start(bf16[1024,128]{1,0:T(8,128)(2,1)} %param.12) | copy-start | bytes 786436
  0.0 22.7 %copy-start = (bf16[512,128]{1,0:T(8,128)(2,1)S(1)}, bf16[512,128]{1,0:T(8,128)(2,1)}, u32[]{:S(2)}) copy-start(bf16[512,128]{1,0:T(8,128)(2,1)} %param.14) | copy-start | bytes 393220
  0.0 22.7 %copy-start.7 = (f32[32,192]{1,0:T(8,128)S(1)}, f32[32,192]{1,0:T(8,128)}, u32[]{:S(2)}) copy-start(f32[32,192]{1,0:T(8,128)} %param.15) | copy-start | bytes 73732
  0.0 22.7 %copy-start.3 = (bf16[64,3072]{1,0:T(8,128)(2,1)S(1)}, bf16[64,3072]{1,0:T(8,128)(2,1)}, u32[]{:S(2)}) copy-start(bf16[64,3072]{1,0:T(8,128)(2,1)} %param.10) | copy-start | bytes 1179652
  0.0 23.4 %copy-start.8 = (f32[32,128]{1,0:T(8,128)S(1)}, f32[32,128]{1,0:T(8,128)}, u32[]{:S(2)}) copy-start(f32[32,128]{1,0:T(8,128)} %param.16) | copy-start | bytes 49156
  0.0 25.2 %copy-start.9 = (bf16[64,48]{0,1:T(8,128)(2,1)S(1)}, bf16[64,48]{0,1:T(8,128)(2,1)}, u32[]{:S(2)}) copy-start(bf16[64,48]{0,1:T(8,128)(2,1)} %param.17) | copy-start | bytes 18436
  3.0 49.8 %collective-permute-start = (bf16[16,192]{1,0:T(8,128)(2,1)}, bf16[16,192]{1,0:T(8,128)(2,1)}, u32[]{:S(2)}, u32[]{:S(2)}) collective-permute-start(bf16[16,192]{1,0:T(8,128)(2,1)} %get-tuple-element.13), channel_id=1, source_target_pairs={{0,24},{8,0},{16,8},{24,16},{1,25},{9,1},{17,9},{25,17},{2,26},{10... | collective-permute-start | bytes 18440 | tf_op jit(solution)/shard_map/ppermute | solution.py:21
  8.0 45.7 %collective-permute-start.1 = (bf16[16,192]{1,0:T(8,128)(2,1)}, bf16[16,192]{1,0:T(8,128)(2,1)}, u32[]{:S(2)}, u32[]{:S(2)}) collective-permute-start(bf16[16,192]{1,0:T(8,128)(2,1)} %get-tuple-element.14), channel_id=1, source_target_pairs={{0,24},{8,0},{16,8},{24,16},{1,25},{9,1},{17,9},{25,17},{2,26},{10... | collective-permute-start | bytes 18440 | tf_op jit(solution)/shard_map/ppermute | solution.py:21
  9.8 25.8 %collective-permute-start.2 = (bf16[16,128]{1,0:T(8,128)(2,1)}, bf16[16,128]{1,0:T(8,128)(2,1)}, u32[]{:S(2)}, u32[]{:S(2)}) collective-permute-start(bf16[16,128]{1,0:T(8,128)(2,1)} %get-tuple-element.15), channel_id=1, source_target_pairs={{0,24},{8,0},{16,8},{24,16},{1,25},{9,1},{17,9},{25,17},{2,26},{10... | collective-permute-start | bytes 12296 | tf_op jit(solution)/shard_map/ppermute | solution.py:21
  10.2 28.2 %collective-permute-start.3 = (bf16[16,128]{1,0:T(8,128)(2,1)}, bf16[16,128]{1,0:T(8,128)(2,1)}, u32[]{:S(2)}, u32[]{:S(2)}) collective-permute-start(bf16[16,128]{1,0:T(8,128)(2,1)} %get-tuple-element.16), channel_id=1, source_target_pairs={{0,24},{8,0},{16,8},{24,16},{1,25},{9,1},{17,9},{25,17},{2,26},{10... | collective-permute-start | bytes 12296 | tf_op jit(solution)/shard_map/ppermute | solution.py:21
  13.7 13.6 %all-to-all-start = ((s32[1,4,4]{1,0,2:T(1,128)}), s32[1,4,4]{1,0,2:T(1,128)S(1)}, u32[]{:S(2)}, u32[]{:S(2)}) async-start(s32[1,4,4]{1,0,2:T(1,128)} %copy.85), calls=%async_computation | async-start | bytes 4096 | tf_op jit(solution)/shard_map/all_to_all | solution.py:135
  19.9 54.4 %collective-permute-start.4 = (bf16[256,192]{0,1:T(8,128)(2,1)S(1)}, bf16[256,192]{0,1:T(8,128)(2,1)}, u32[]{:S(2)}, u32[]{:S(2)}) collective-permute-start(bf16[256,192]{0,1:T(8,128)(2,1)S(1)} %slice_select_fusion), channel_id=1, source_target_pairs={{0,8},{8,16},{16,24},{24,0},{1,9},{9,17},{17,25},{25,1},{2,10},{10... | collective-permute-start | bytes 294920 | tf_op jit(solution)/shard_map/ppermute | solution.py:21
  31.1 39.6 %all-to-all-start.2 = ((bf16[1,4,4,64,128]{4,3,1,0,2:T(8,128)(2,1)}), bf16[1,4,4,64,128]{4,3,1,0,2:T(8,128)(2,1)S(1)}, u32[]{:S(2)}, u32[]{:S(2)}) async-start(bf16[1,4,4,64,128]{4,3,1,0,2:T(8,128)(2,1)} %copy.95), calls=%async_computation.2 | async-start | bytes 524288 | tf_op jit(solution)/shard_map/all_to_all | solution.py:153
  35.6 40.8 %collective-permute-start.5 = (bf16[256,128]{1,0:T(8,128)(2,1)S(1)}, bf16[256,128]{1,0:T(8,128)(2,1)}, u32[]{:S(2)}, u32[]{:S(2)}) collective-permute-start(bf16[256,128]{1,0:T(8,128)(2,1)S(1)} %slice_select_fusion.1), channel_id=1, source_target_pairs={{0,8},{8,16},{16,24},{24,0},{1,9},{9,17},{17,25},{25,1},{2,10},{10... | collective-permute-start | bytes 196616 | tf_op jit(solution)/shard_map/ppermute | solution.py:21
  54.6 14.4 %copy-start.10 = (s32[384]{0:T(512)S(1)}, s32[384]{0:T(512)}, u32[]{:S(2)}) copy-start(s32[384]{0:T(512)} %multiply_add_fusion) | copy-start | bytes 4612
  70.5 3.8 %copy-start.2 = (bf16[512,192]{0,1:T(8,128)(2,1)S(1)}, bf16[512,192]{0,1:T(8,128)(2,1)}, u32[]{:S(2)}) copy-start(bf16[512,192]{0,1:T(8,128)(2,1)} %param.13) | copy-start | bytes 589828
  70.6 13.7 %all-to-all-start.1 = ((bf16[1,4,4,64,192]{4,3,1,0,2:T(8,128)(2,1)}), bf16[1,4,4,64,192]{4,3,1,0,2:T(8,128)(2,1)S(1)}, u32[]{:S(2)}, u32[]{:S(2)}) async-start(bf16[1,4,4,64,192]{4,3,1,0,2:T(8,128)(2,1)} %copy_select_fusion), calls=%async_computation.1 | async-start | bytes 1048576 | tf_op jit(solution)/shard_map/all_to_all | solution.py:152
  77.9 6.5 %copy-start.11 = (pred[1024]{0:T(1024)(128)(4,1)S(1)}, pred[1024]{0:T(1024)(128)(4,1)}, u32[]{:S(2)}) copy-start(pred[1024]{0:T(1024)(128)(4,1)} %and.99) | copy-start | bytes 3076
  87.5 2.0 %copy-start.4 = (f32[64,16]{1,0:T(8,128)S(1)}, f32[64,16]{1,0:T(8,128)}, u32[]{:S(2)}) copy-start(f32[64,16]{1,0:T(8,128)} %copy.76) | copy-start | bytes 12292
  89.4 0.8 copy-start.5
  89.4 0.9 %copy-start.6 = (f32[64,16]{1,0:T(8,128)S(1)}, f32[64,16]{1,0:T(8,128)}, u32[]{:S(2)}) copy-start(f32[64,16]{1,0:T(8,128)} %copy.97) | copy-start | bytes 12292
where the time goes:
time: 92.6 us; the launch traced here: 91.8 us
  blocking collectives  26.8 us (29%)
  starting transfers between devices  22.7 us (25%)
  other arithmetic  14.1 us (15%)
  local copies, waits for them, and re-layouts  13.3 us (14%)
  matrix products  7.31 us (8%)
  waiting for transfers between devices  6.38 us (7%)
  between operations  1.25 us (1%)
    all_gather x1, blocking collectives, local(): part_keys = lax.all_gather(summary_keys, 'ctx', axis=0, tiled=True)  13.6 us
    all_gather x1, blocking collectives, local(): part_values = lax.all_gather(summary_values, 'ctx', axis=0, tiled=True)  13.2 us
    ppermute x6, starting transfers between devices, from_behind(): return lax.ppermute(value, axis, pairs)  10.1 us
    all_to_all x1, waiting for transfers between devices, local(): lax.all_to_all(served_keys, 'ctx', split_axis=2, concat_axis=2, tiled=True)  6.36 us
    all_to_all x1, starting transfers between devices, local(): lax.all_to_all(requested, 'ctx', split_axis=2, concat_axis=2, tiled=True)  5.27 us
    all_to_all x1, starting transfers between devices, local(): lax.all_to_all(served_keys, 'ctx', split_axis=2, concat_axis=2, tiled=True)  3.66 us
    all_to_all x1, starting transfers between devices, local(): lax.all_to_all(served_values, 'ctx', split_axis=2, concat_axis=2, tiled=T...  3.63 us
    unnamed x27, local copies, waits for them, and re-layouts  3.33 us
  transfers between devices with their start and end apart: 9, of which 1 were waited for; matrix products, arithmetic and copies ran while one was open for 27% of the time, Pallas kernels for 0%

commit v1 on v0

v1 whole, which is shorter than its diff:
```python
import functools
import math

import jax
import jax.numpy as jnp
import numpy as np
from jax import lax
from jax.experimental import pallas as pl
from jax.experimental.pallas import tpu as pltpu
from jax.sharding import PartitionSpec as P

HEADS = 16
CLEN = 32
STRIDE = 16
BLOCK = 64
HALF = BLOCK // 2
WINDOW = 256
NEG_FILL = -1e30
LANES = 128
GROUP = 4
MESH = pl.DeviceIdType.MESH
F32 = jnp.float32
BF16 = jnp.bfloat16


def pool_rows(rows, extra, weights):
    count, width = rows.shape[0] // STRIDE, rows.shape[1]
    grouped = rows.astype(F32).reshape(count, STRIDE, width)
    leading = jnp.sum(grouped * weights[None, :STRIDE, :], axis=1)
    trailing = jnp.sum(grouped * weights[None, STRIDE:, :], axis=1)
    after = jnp.sum(extra.astype(F32) * weights[STRIDE:, :], axis=0, keepdims=True)
    trailing = jnp.concatenate([trailing[1:], after], axis=0)
    return (leading + trailing).astype(BF16)


def kernel(
    n,
    m,
    queries,
    cache_keys,
    cache_values,
    span_keys,
    span_values,
    pool_keys,
    pool_values,
    gate_logits,
    comp_ends,
    chosen,
    valid,
    out,
    q_in,
    ck,
    cv,
    rk,
    rv,
    packed,
    comp,
    comp_k,
    comp_v,
    heads_k,
    heads_v,
    qa,
    qb,
    sel_k,
    sel_v,
    gates,
    acc,
    bias_comp,
    bias_sel,
    bias_win,
    local_sem,
    head_send,
    head_recv,
    tail_send,
    tail_recv,
    z_send,
    z_recv,
    p_send,
    p_recv,
    s_send,
    s_recv,
    cz_send,
    cz_recv,
    cs_send,
    cs_recv,
):
    c, p, r = lax.axis_index("ctx"), lax.axis_index("pb"), lax.axis_index("row")
    place = p * 2 + r
    cache_len, dk = ck.shape
    span_len = span_keys.shape[0]
    tokens = q_in.shape[0]
    blocks = cache_len // BLOCK
    piece = blocks // (2 * m)
    cache_half, span_half = cache_len // 2, span_len // 2
    comp_cache = cache_half // STRIDE
    picks = chosen.shape[1]
    scale = 1.0 / math.sqrt(dk)
    before, after = lax.rem(c + n - 1, n), lax.rem(c + 1, n)
    tail_parts = WINDOW // BLOCK

    def remote(src, dst, send, recv, ctx=None, pb=None, row=None):
        target = {
            "ctx": c if ctx is None else ctx,
            "pb": p if pb is None else pb,
            "row": r if row is None else row,
        }
        return pltpu.make_async_remote_copy(
            src_ref=src, dst_ref=dst, send_sem=send, recv_sem=recv,
            device_id=target, device_id_type=MESH,
        )

    own_copies = [
        pltpu.make_async_copy(cache_keys, ck, local_sem.at[0]),
        pltpu.make_async_copy(cache_values, cv, local_sem.at[1]),
        pltpu.make_async_copy(span_keys, rk.at[pl.ds(WINDOW, span_len)], local_sem.at[2]),
        pltpu.make_async_copy(span_values, rv.at[pl.ds(WINDOW, span_len)], local_sem.at[3]),
        pltpu.make_async_copy(queries, q_in, local_sem.at[4]),
    ]
    for copy in own_copies:
        copy.start()

    barrier = pltpu.get_barrier_semaphore()
    for k in range(1, n):
        pl.semaphore_signal(
            barrier, inc=1, device_id={"ctx": lax.rem(c + k, n), "pb": p, "row": r},
            device_id_type=MESH,
        )
    for j in range(1, m):
        pl.semaphore_signal(
            barrier, inc=1, device_id={"ctx": c, "pb": lax.rem(p + j, m), "row": r},
            device_id_type=MESH,
        )
    pl.semaphore_signal(
        barrier, inc=1, device_id={"ctx": c, "pb": p, "row": 1 - r}, device_id_type=MESH
    )

    own_copies[0].wait()
    own_copies[1].wait()
    for b in range(blocks):
        low, mid, high = b * BLOCK, b * BLOCK + HALF, (b + 1) * BLOCK
        spot = c * blocks + b
        packed[spot, 0:BLOCK, :] = ck[low:high, :LANES]
        packed[spot, BLOCK : 2 * BLOCK, :] = cv[low:high, :]
        packed[spot, 2 * BLOCK : 2 * BLOCK + HALF, :] = jnp.concatenate(
            [ck[low:mid, LANES:], ck[mid:high, LANES:]], axis=1
        )
    pl.semaphore_wait(barrier, n + m - 1)

    def head_copies(keys, values):
        return [
            remote(keys.at[pl.ds(0, STRIDE)], heads_k.at[0], head_send.at[0], head_recv.at[0], ctx=before),
            remote(values.at[pl.ds(0, STRIDE)], heads_v.at[0], head_send.at[1], head_recv.at[1], ctx=before),
            remote(span_keys.at[pl.ds(0, STRIDE)], heads_k.at[1], head_send.at[2], head_recv.at[2], ctx=before),
            remote(span_values.at[pl.ds(0, STRIDE)], heads_v.at[1], head_send.at[3], head_recv.at[3], ctx=before),
        ]

    @pl.when((r == 1) & (c == 0))
    def _():
        for copy in head_copies(span_keys, span_values):
            copy.start()

    @pl.when((r == 1) & (c != 0))
    def _():
        for copy in head_copies(cache_keys, cache_values):
            copy.start()

    def z_copy(k, owner, target):
        spot = packed.at[pl.ds(owner * blocks + place * piece, piece)]
        return remote(spot, spot, z_send.at[k - 1], z_recv.at[k - 1], ctx=target)

    for k in range(1, n):
        z_copy(k, c, lax.rem(c + n - k, n)).start()

    own_copies[2].wait()
    own_copies[3].wait()

    @pl.when(r == 0)
    def _():
        heads_k[0] = ck[cache_half : cache_half + STRIDE, :]
        heads_v[0] = cv[cache_half : cache_half + STRIDE, :]
        heads_k[1] = rk[WINDOW + span_half : WINDOW + span_half + STRIDE, :]
        heads_v[1] = rv[WINDOW + span_half : WINDOW + span_half + STRIDE, :]

    @pl.when(r == 1)
    def _():
        for copy in head_copies(cache_keys, cache_values):
            copy.wait()

    cache_low = pl.multiple_of(r * cache_half, cache_half)
    span_low = pl.multiple_of(WINDOW + r * span_half, 64)
    weights_k, weights_v = pool_keys[...], pool_values[...]
    comp[c, r, 1] = jnp.zeros(comp.shape[3:], BF16)
    pooled = pool_rows(ck[pl.ds(cache_low, cache_half), :], heads_k[0], weights_k)
    comp[c, r, 0, 0:comp_cache, :] = pooled[:, :LANES]
    comp[c, r, 1, 0:comp_cache, 0 : dk - LANES] = pooled[:, LANES:]
    pooled = pool_rows(rk[pl.ds(span_low, span_half), :], heads_k[1], weights_k)
    comp[c, r, 0, comp_cache:, :] = pooled[:, :LANES]
    comp[c, r, 1, comp_cache:, 0 : dk - LANES] = pooled[:, LANES:]
    comp[c, r, 2, 0:comp_cache, :] = pool_rows(
        cv[pl.ds(cache_low, cache_half), :], heads_v[0], weights_v
    )
    comp[c, r, 2, comp_cache:, :] = pool_rows(
        rv[pl.ds(span_low, span_half), :], heads_v[1], weights_v
    )

    def comp_z(k, owner, target):
        spot = comp.at[owner, r]
        return remote(spot, spot, cz_send.at[k - 1], cz_recv.at[k - 1], ctx=target)

    def comp_s(k, owner, row):
        spot = comp.at[owner, row]
        return remote(spot, spot, cs_send.at[k], cs_recv.at[k], row=1 - r)

    for k in range(1, n):
        comp_z(k, c, lax.rem(c + n - k, n)).start()
    comp_s(0, c, r).start()

    def tail_copies(keys, values, part):
        rows = keys.shape[0]
        source = pl.ds(rows - WINDOW + part * BLOCK, BLOCK)
        dest = pl.ds(part * BLOCK, BLOCK)
        return [
            remote(keys.at[source], rk.at[dest], tail_send.at[part, 0], tail_recv.at[part, 0], ctx=after),
            remote(values.at[source], rv.at[dest], tail_send.at[part, 1], tail_recv.at[part, 1], ctx=after),
        ]

    for part in range(tail_parts):

        @pl.when((place * tokens <= part * BLOCK) & (c == n - 1))
        def _():
            for copy in tail_copies(cache_keys, cache_values, part):
                copy.start()

        @pl.when((place * tokens <= part * BLOCK) & (c != n - 1))
        def _():
            for copy in tail_copies(span_keys, span_values, part):
                copy.start()

    def p_copy(k, j, from_pb, target):
        owner = lax.rem(c + k, n)
        spot = packed.at[pl.ds(owner * blocks + (from_pb * 2 + r) * piece, piece)]
        at = (k - 1) * (m - 1) + j - 1
        return remote(spot, spot, p_send.at[at], p_recv.at[at], pb=target)

    def s_copy(k, j, row):
        owner = lax.rem(c + k, n)
        from_pb = lax.rem(p + m - j, m)
        spot = packed.at[pl.ds(owner * blocks + (from_pb * 2 + row) * piece, piece)]
        at = (k - 1) * m + j
        return remote(spot, spot, s_send.at[at], s_recv.at[at], row=1 - r)

    def forward(k):
        z_copy(k, lax.rem(c + k, n), lax.rem(c + k, n)).wait_recv()
        for j in range(1, m):
            p_copy(k, j, p, lax.rem(p + j, m)).start()
        s_copy(k, 0, r).start()

    def share(k):
        for j in range(1, m):
            p_copy(k, j, lax.rem(p + m - j, m), lax.rem(p + m - j, m)).wait_recv()
            s_copy(k, j, r).start()

    own_copies[4].wait()
    blank = jnp.zeros((tokens, 2 * LANES - dk), BF16)
    for h in range(HEADS):
        low = h * dk
        first, last = q_in[:, low : low + LANES], q_in[:, low + LANES : low + dk]
        rows = pl.ds(h * tokens, tokens)
        qa[rows, 0:LANES] = first
        qb[rows, 0:LANES] = first
        qa[rows, LANES:] = jnp.concatenate([last, blank], axis=1)
        qb[rows, LANES:] = jnp.concatenate([blank, last], axis=1)

    forward(1)

    sigmoid = jax.nn.sigmoid(gate_logits[...].astype(F32))
    for g in range(3):
        for h in range(HEADS):
            column = g * HEADS + h
            gates[g, h * tokens : (h + 1) * tokens, :] = jnp.broadcast_to(
                sigmoid[:, column : column + 1], (tokens, LANES)
            )

    first_pos = n * cache_len + c * span_len + place * tokens
    def token_lane(width):
        return (
            lax.broadcasted_iota(jnp.int32, (tokens, width), 0),
            lax.broadcasted_iota(jnp.int32, (tokens, width), 1),
        )

    token, lane = token_lane(bias_win.shape[1])
    bias_win[...] = jnp.where((lane <= token + WINDOW) & (lane > token), 0.0, NEG_FILL)
    token, lane = token_lane(bias_comp.shape[1])
    bias_comp[...] = jnp.where(comp_ends[...] <= token + (first_pos + 1), 0.0, NEG_FILL)
    token, lane = token_lane(bias_sel.shape[1])
    in_half = picks * HALF
    second = (lane >= in_half).astype(jnp.int32)
    slot = (lane - second * in_half) >> int(math.log2(HALF))
    offset = (lane & (HALF - 1)) + second * HALF
    seen = (slot < valid[0]) & ((slot > 0) | (offset <= token))
    bias_sel[...] = jnp.where(seen, 0.0, NEG_FILL)

    group_rows = GROUP * tokens

    def softmax_out(scores, bias, values):
        width = scores.shape[1]
        scores = (scores * scale).reshape(GROUP, tokens, width) + bias[None]
        scores = scores.reshape(group_rows, width)
        highest = jnp.max(scores, axis=1, keepdims=True)
        exponent = jnp.exp(scores - highest)
        total = jnp.sum(exponent, axis=1, keepdims=True)
        numerator = jnp.dot(exponent.astype(BF16), values, preferred_element_type=F32)
        return numerator / total

    def dot_t(a, b):
        return lax.dot_general(a, b, (((1,), (1,)), ((), ())), preferred_element_type=F32)

    for k in range(2, min(3, n)):
        forward(k)

    for part in range(tail_parts):

        @pl.when(place * tokens <= part * BLOCK)
        def _():
            for copy in tail_copies(span_keys, span_values, part):
                copy.wait()

    near = pl.ds(pl.multiple_of(place * tokens, tokens), WINDOW + tokens)

    @pl.loop(0, HEADS // GROUP)
    def _(g):
        rows = pl.ds(pl.multiple_of(g * group_rows, group_rows), group_rows)
        scores = dot_t(qa[rows, 0:dk], rk[near, :])
        acc[rows, :] = gates[2, rows, :] * softmax_out(scores, bias_win[...], rv[near, :])

    for k in range(3, n):
        forward(k)

    comp_s(0, c, 1 - r).wait_recv()
    for k in range(1, n):
        owner = lax.rem(c + k, n)
        comp_z(k, owner, owner).wait_recv()
        comp_s(k, owner, r).start()
    share(1)
    for k in range(1, n):
        comp_s(k, lax.rem(c + k, n), 1 - r).wait_recv()
    part_rows = comp.shape[3]
    for owner in range(n):
        for row in range(2):
            low = (owner * 2 + row) * part_rows
            comp_k[low : low + part_rows, 0:LANES] = comp[owner, row, 0]
            comp_k[low : low + part_rows, LANES:] = comp[owner, row, 1]
            comp_v[low : low + part_rows, :] = comp[owner, row, 2]

    @pl.loop(0, HEADS // GROUP)
    def _(g):
        rows = pl.ds(pl.multiple_of(g * group_rows, group_rows), group_rows)
        scores = dot_t(qa[rows, :], comp_k[...])
        acc[rows, :] += gates[0, rows, :] * softmax_out(scores, bias_comp[...], comp_v[...])

    for k in range(2, n):
        share(k)
    for k in range(1, n):
        for j in range(m):
            s_copy(k, j, 1 - r).wait_recv()

    own = pl.multiple_of(WINDOW + place * tokens, tokens)
    own_k, own_v = rk[pl.ds(own, BLOCK), :], rv[pl.ds(own, BLOCK), :]
    own_tail = jnp.concatenate([own_k[:HALF, LANES:], own_k[HALF:, LANES:]], axis=1)
    for s in range(picks):
        if s == 0:
            key_rows, value_rows, tail = own_k[:, :LANES], own_v, own_tail
        else:
            number = chosen[0, s]
            key_rows = packed[number, 0:BLOCK, :]
            value_rows = packed[number, BLOCK : 2 * BLOCK, :]
            tail = packed[number, 2 * BLOCK : 2 * BLOCK + HALF, :]
        for part in range(2):
            low = part * in_half + s * HALF
            sel_k[low : low + HALF, 0:LANES] = key_rows[part * HALF : (part + 1) * HALF]
            sel_k[low : low + HALF, LANES:] = tail
            sel_v[low : low + HALF, :] = value_rows[part * HALF : (part + 1) * HALF]

    @pl.loop(0, HEADS // GROUP)
    def _(g):
        rows = pl.ds(pl.multiple_of(g * group_rows, group_rows), group_rows)
        scores = jnp.concatenate(
            [dot_t(qa[rows, :], sel_k[0:in_half, :]), dot_t(qb[rows, :], sel_k[in_half:, :])], axis=1
        )
        mixed = acc[rows, :] + gates[1, rows, :] * softmax_out(scores, bias_sel[...], sel_v[...])
        for i in range(GROUP):
            column = pl.multiple_of((g * GROUP + i) * LANES, LANES)
            out[:, pl.ds(column, LANES)] = mixed[i * tokens : (i + 1) * tokens].astype(BF16)

    for k in range(1, n):
        z_copy(k, c, lax.rem(c + n - k, n)).wait_send()
        comp_z(k, c, lax.rem(c + n - k, n)).wait_send()
        for j in range(1, m):
            p_copy(k, j, p, lax.rem(p + j, m)).wait_send()
        for j in range(m):
            s_copy(k, j, r).wait_send()
    for k in range(n):
        comp_s(k, lax.rem(c + k, n), r).wait_send()


def local(
    queries,
    cache_keys,
    cache_values,
    span_keys,
    span_values,
    pool_keys,
    pool_values,
    gate_logits,
    chosen_blocks,
    valid_counts,
):
    n, m = lax.axis_size("ctx"), lax.axis_size("pb")
    tokens = queries.shape[0]
    cache_len, dk = cache_keys.shape
    dv = cache_values.shape[1]
    span_len = span_keys.shape[0]
    rows = tokens * HEADS
    picks = chosen_blocks.shape[1]
    comp_cache, comp_span = cache_len // 2 // STRIDE, span_len // 2 // STRIDE
    part_rows = comp_cache + comp_span
    shares = np.arange(n * 2)[:, None]
    ids = np.concatenate(
        [
            shares * comp_cache + np.arange(comp_cache)[None],
            2 * n * comp_cache + shares * comp_span + np.arange(comp_span)[None],
        ],
        axis=1,
    ).reshape(1, -1)
    comp_ends = jnp.asarray(ids * STRIDE + CLEN, dtype=jnp.int32)
    blocks = cache_len // BLOCK
    sem = pltpu.SemaphoreType.DMA
    anywhere = pl.BlockSpec(memory_space=pl.ANY)
    vmem = pl.BlockSpec(memory_space=pltpu.VMEM)
    smem = pl.BlockSpec(memory_space=pltpu.SMEM)
    keys = n * 2 * part_rows + picks * BLOCK + WINDOW + tokens
    return pl.pallas_call(
        functools.partial(kernel, n, m),
        out_shape=jax.ShapeDtypeStruct((tokens, HEADS * dv), BF16),
        in_specs=[anywhere] * 5 + [vmem] * 4 + [smem] * 2,
        out_specs=vmem,
        scratch_shapes=[
            pltpu.VMEM((tokens, HEADS * dk), BF16),
            pltpu.VMEM((cache_len, dk), BF16),
            pltpu.VMEM((cache_len, dv), BF16),
            pltpu.VMEM((WINDOW + span_len, dk), BF16),
            pltpu.VMEM((WINDOW + span_len, dv), BF16),
            pltpu.VMEM((n * blocks, 2 * BLOCK + HALF, LANES), BF16),
            pltpu.VMEM((n, 2, 3, part_rows, LANES), BF16),
            pltpu.VMEM((n * 2 * part_rows, 2 * LANES), BF16),
            pltpu.VMEM((n * 2 * part_rows, dv), BF16),
            pltpu.VMEM((2, STRIDE, dk), BF16),
            pltpu.VMEM((2, STRIDE, dv), BF16),
            pltpu.VMEM((rows, 2 * LANES), BF16),
            pltpu.VMEM((rows, 2 * LANES), BF16),
            pltpu.VMEM((picks * BLOCK, 2 * LANES), BF16),
            pltpu.VMEM((picks * BLOCK, dv), BF16),
            pltpu.VMEM((3, rows, LANES), F32),
            pltpu.VMEM((rows, dv), F32),
            pltpu.VMEM((tokens, n * 2 * part_rows), F32),
            pltpu.VMEM((tokens, picks * BLOCK), F32),
            pltpu.VMEM((tokens, WINDOW + tokens), F32),
            sem((5,)),
            sem((4,)),
            sem((4,)),
            sem((WINDOW // BLOCK, 2)),
            sem((WINDOW // BLOCK, 2)),
            sem((n - 1,)),
            sem((n - 1,)),
            sem(((n - 1) * (m - 1),)),
            sem(((n - 1) * (m - 1),)),
            sem(((n - 1) * m,)),
            sem(((n - 1) * m,)),
            sem((n - 1,)),
            sem((n - 1,)),
            sem((n,)),
            sem((n,)),
        ],
        compiler_params=pltpu.CompilerParams(
            collective_id=0, has_side_effects=True, vmem_limit_bytes=48 * 1024 * 1024
        ),
        cost_estimate=pl.CostEstimate(
            flops=2 * rows * keys * (dk + dv),
            bytes_accessed=4 * 1024 * 1024,
            transcendentals=rows * keys,
        ),
    )(
        queries,
        cache_keys,
        cache_values,
        span_keys,
        span_values,
        pool_keys,
        pool_values,
        gate_logits,
        comp_ends,
        chosen_blocks,
        valid_counts,
    )


def solution(mesh):
    spread = P(("parts", "ctx", "pb", "row"), None)
    shard = P(("parts", "ctx"), None)
    return jax.shard_map(
        local,
        mesh=mesh,
        in_specs=(
            spread,
            shard,
            shard,
            shard,
            shard,
            P(),
            P(),
            spread,
            spread,
            P(("parts", "ctx", "pb", "row")),
        ),
        out_specs=spread,
        check_vma=False,
    )
```

time: 92.6 us -> 36.4 us (0.39)
  Pallas kernels: 0 us -> 31.8 us
  blocking collectives: 26.8 us -> 0 us
  starting transfers between devices: 22.7 us -> 0 us
  other arithmetic: 14.1 us -> 0 us
  local copies, waits for them, and re-layouts: 13.3 us -> 3.62 us
  matrix products: 7.31 us -> 0 us
  waiting for transfers between devices: 6.38 us -> 0 us
    pallas_call x0 -> x1, Pallas kernels: none -> 31.8 us  [local(): pl.pallas_call(functools.partial(kernel, n, m), out_shape=jax.ShapeDtypeS...]
    all_gather x2 -> x0, blocking collectives: 26.8 us -> none  [the longest x1 13.6 us: local(): part_keys = lax.all_gather(summary_keys, 'ctx', axis=0, tiled=True)]
    all_to_all x3 -> x0, starting transfers between devices: 12.6 us -> none  [the longest x1 5.27 us: local(): lax.all_to_all(requested, 'ctx', split_axis=2, concat_axis=2, tiled=True)]
    ppermute x6 -> x0, starting transfers between devices: 10.1 us -> none  [from_behind(): return lax.ppermute(value, axis, pairs)]
    dot_general x6 -> x0, matrix products: 7.31 us -> none  [the longest x2 3.33 us: attend(): numerator = jnp.dot(weights, values, preferred_element_type=jnp.float32)]
    all_to_all x3 -> x0, waiting for transfers between devices: 6.36 us -> none  [the longest x1 6.36 us: local(): lax.all_to_all(served_keys, 'ctx', split_axis=2, concat_axis=2, tiled=True)]
    convert_element_type x9 -> x0, other arithmetic: 4.23 us -> none  [the longest x4 2.93 us: pool_blocks(): joined = jnp.concatenate([rows, extra], axis=0).astype(jnp.float32)]
    select_n x10 -> x0, other arithmetic: 3.9 us -> none  [the longest x1 1.29 us: local(): jnp.where(leader, span_values[:STRIDE], cache_values[:STRIDE])]
  transfers between devices with their start and end apart: 9 -> 0, of which waited for: 1 -> 0; matrix products, arithmetic and copies ran while one was open for 27% -> 0% of each run, Pallas kernels for 0% -> 0%
where the time goes in v1:
time: 36.4 us; the launch traced here: 36.2 us
  Pallas kernels  31.8 us (87%)
  local copies, waits for them, and re-layouts  3.62 us (10%)
  between operations  0.79 us (2%)
    pallas_call x1, Pallas kernels, local(): pl.pallas_call(functools.partial(kernel, n, m), out_shape=jax.ShapeDtypeS...  31.8 us
    unnamed x20, local copies, waits for them, and re-layouts  3.62 us

profile of v1, /device:TPU:0, one launch (start us, length us, event | category | flops | bytes accessed | tf_op | source)
XLA Modules:
  0.0 36.2 jit_solution(10863128892367304841)
XLA Ops:
  0.0 0.0 copy-start.7
  0.7 0.8 %copy.14.gate_logits = bf16[64,48]{1,0:T(8,128)(2,1)S(1)} copy(bf16[64,48]{0,1:T(8,128)(2,1)} %param.18) | data formatting | bytes 12288 | tf_op args[7]
  1.5 1.1 %copy.13.span_keys = bf16[512,192]{1,0:T(8,128)(2,1)S(1)} copy(bf16[512,192]{0,1:T(8,128)(2,1)} %param.14) | data formatting | bytes 393216 | tf_op args[3]
  2.6 0.0 copy-done.7
  2.6 0.0 copy-start
  2.6 0.0 copy-start.1
  2.6 0.0 copy-start.2
  2.6 0.0 copy-start.3
  2.6 0.0 copy-start.4
  2.6 0.0 copy-start.5
  2.7 0.0 copy-start.6
  2.7 0.2 copy.12.cache_keys
  2.9 0.7 %copy-done = bf16[64,3072]{1,0:T(8,128)(2,1)S(1)} copy-done((bf16[64,3072]{1,0:T(8,128)(2,1)S(1)}, bf16[64,3072]{1,0:T(8,128)(2,1)}, u32[]{:S(2)}) %copy-start) | copy-done | bytes 393240
  3.6 0.1 copy-done.1
  3.7 0.0 copy-done.2
  3.7 0.0 copy-done.3
  3.7 0.0 copy-done.4
  3.7 0.0 copy-done.5
  3.7 0.0 copy-done.6
  3.7 31.8 %shard_map.109 = bf16[64,2048]{1,0:T(8,128)(2,1)S(1)} custom-call(bf16[64,3072]{1,0:T(8,128)(2,1)S(1)} %copy-done, bf16[1024,192]{1,0:T(8,128)(2,1)S(1)} %copy.12.cache_keys, bf16[1024,128]{1,0:T(8,128)(2,1)S(1)} %copy-done.1, bf16[512,192]{1,0:T(8,128)(2,1)S(1)} %copy.13.span_keys, bf16[512,128]{1,0:T(8,128)(2,1)S(1)} %copy-done.2, ...), custom_call_target="tpu_custom_call" | custom-call | flops 1132462080 | bytes 4194304 | tf_op jit(solution)/shard_map/pallas_call | solution.py:442
  35.5 0.7 %copy.17 = bf16[64,2048]{1,0:T(8,128)(2,1)} copy(bf16[64,2048]{1,0:T(8,128)(2,1)S(1)} %shard_map.109) | data formatting | bytes 524288
Async XLA Ops:
  0.0 2.6 %copy-start.7 = (bf16[1024,192]{0,1:T(8,128)(2,1)S(1)}, bf16[1024,192]{0,1:T(8,128)(2,1)}, u32[]{:S(2)}) copy-start(bf16[1024,192]{0,1:T(8,128)(2,1)} %param.12) | copy-start | bytes 1179652
  2.6 1.0 %copy-start = (bf16[64,3072]{1,0:T(8,128)(2,1)S(1)}, bf16[64,3072]{1,0:T(8,128)(2,1)}, u32[]{:S(2)}) copy-start(bf16[64,3072]{1,0:T(8,128)(2,1)} %queries.1) | copy-start | bytes 1179652
  2.6 1.1 %copy-start.1 = (bf16[1024,128]{1,0:T(8,128)(2,1)S(1)}, bf16[1024,128]{1,0:T(8,128)(2,1)}, u32[]{:S(2)}) copy-start(bf16[1024,128]{1,0:T(8,128)(2,1)} %cache_values.1) | copy-start | bytes 786436
  2.6 1.1 %copy-start.2 = (bf16[512,128]{1,0:T(8,128)(2,1)S(1)}, bf16[512,128]{1,0:T(8,128)(2,1)}, u32[]{:S(2)}) copy-start(bf16[512,128]{1,0:T(8,128)(2,1)} %span_values.1) | copy-start | bytes 393220
  2.6 1.1 %copy-start.3 = (f32[32,192]{1,0:T(8,128)S(1)}, f32[32,192]{1,0:T(8,128)}, u32[]{:S(2)}) copy-start(f32[32,192]{1,0:T(8,128)} %pool_keys.1) | copy-start | bytes 73732
  2.6 1.1 %copy-start.4 = (f32[32,128]{1,0:T(8,128)S(1)}, f32[32,128]{1,0:T(8,128)}, u32[]{:S(2)}) copy-start(f32[32,128]{1,0:T(8,128)} %pool_values.1) | copy-start | bytes 49156
  2.6 1.1 %copy-start.5 = (s32[1,16]{1,0:T(1,128)S(1)}, s32[1,16]{1,0:T(1,128)}, u32[]{:S(2)}) copy-start(s32[1,16]{1,0:T(1,128)} %chosen.1) | copy-start | bytes 196
  2.7 1.0 %copy-start.6 = (s32[1,384]{1,0:T(1,128)S(1)}, s32[1,384]{1,0:T(1,128)}, u32[]{:S(2)}) copy-start(s32[1,384]{1,0:T(1,128)} %constant.2.clone.comp_ends) | copy-start | bytes 4612

commit v2 on v1

v2 whole, which is shorter than its diff:
```python
import functools
import math

import jax
import jax.numpy as jnp
import numpy as np
from jax import lax
from jax.experimental import pallas as pl
from jax.experimental.pallas import tpu as pltpu
from jax.sharding import PartitionSpec as P

HEADS = 16
CLEN = 32
STRIDE = 16
BLOCK = 64
WINDOW = 256
NEG_FILL = -1e30
LANES = 128
GROUP = 16
MESH = pl.DeviceIdType.MESH
F32 = jnp.float32
BF16 = jnp.bfloat16


def pool_rows(rows, extra, weights):
    count, width = rows.shape[0] // STRIDE, rows.shape[1]
    grouped = rows.astype(F32).reshape(count, STRIDE, width)
    leading = jnp.sum(grouped * weights[None, :STRIDE, :], axis=1)
    trailing = jnp.sum(grouped * weights[None, STRIDE:, :], axis=1)
    after = jnp.sum(extra.astype(F32) * weights[STRIDE:, :], axis=0, keepdims=True)
    trailing = jnp.concatenate([trailing[1:], after], axis=0)
    return (leading + trailing).astype(BF16)


def kernel(
    n,
    m,
    queries,
    cache_keys,
    cache_values,
    span_keys,
    span_values,
    pool_keys,
    pool_values,
    gate_logits,
    comp_ends,
    chosen,
    valid,
    out,
    q_in,
    packed,
    near,
    comp,
    comp_k,
    comp_v,
    lead_k,
    lead_v,
    heads_k,
    heads_v,
    qa,
    sel_k,
    sel_v,
    gates,
    acc,
    bias_comp,
    bias_sel,
    bias_win,
    q_sem,
    cache_sem,
    span_sem,
    head_send,
    head_recv,
    tail_send,
    tail_recv,
    pair_send,
    pair_recv,
    z_send,
    z_recv,
    p_send,
    p_recv,
    s_send,
    s_recv,
    cz_send,
    cz_recv,
    cs_send,
    cs_recv,
):
    c, p, r = lax.axis_index("ctx"), lax.axis_index("pb"), lax.axis_index("row")
    place = p * 2 + r
    dk, cache_len = cache_keys.shape
    span_len = span_keys.shape[1]
    tokens = q_in.shape[0]
    tiles, span_tiles, tail_tiles = cache_len // LANES, span_len // LANES, WINDOW // LANES
    tile_rows = packed.shape[1]
    comp_cache = cache_len // 2 // STRIDE
    picks = chosen.shape[1]
    scale = 1.0 / math.sqrt(dk)
    before, after = lax.rem(c + n - 1, n), lax.rem(c + 1, n)

    def remote(src, dst, send, recv, ctx=None, pb=None, row=None):
        target = {
            "ctx": c if ctx is None else ctx,
            "pb": p if pb is None else pb,
            "row": r if row is None else row,
        }
        return pltpu.make_async_remote_copy(
            src_ref=src, dst_ref=dst, send_sem=send, recv_sem=recv,
            device_id=target, device_id_type=MESH,
        )

    cache_copies, span_copies = [], []
    for i in range(tiles):
        lanes, spot = pl.ds(i * LANES, LANES), packed.at[c * tiles + i]
        cache_copies += [
            pltpu.make_async_copy(cache_keys.at[:, lanes], spot.at[pl.ds(0, dk)], cache_sem.at[i, 0]),
            pltpu.make_async_copy(cache_values.at[lanes], spot.at[pl.ds(dk, LANES)], cache_sem.at[i, 1]),
        ]
    for i in range(span_tiles):
        lanes, spot = pl.ds(i * LANES, LANES), near.at[tail_tiles + i]
        span_copies += [
            pltpu.make_async_copy(span_keys.at[:, lanes], spot.at[pl.ds(0, dk)], span_sem.at[i, 0]),
            pltpu.make_async_copy(span_values.at[lanes], spot.at[pl.ds(dk, LANES)], span_sem.at[i, 1]),
        ]
    q_copy = pltpu.make_async_copy(queries, q_in, q_sem.at[0])
    for copy in cache_copies + span_copies + [q_copy]:
        copy.start()

    barrier = pltpu.get_barrier_semaphore()
    for k in range(1, n):
        pl.semaphore_signal(
            barrier, inc=1, device_id={"ctx": lax.rem(c + k, n), "pb": p, "row": r},
            device_id_type=MESH,
        )
    for j in range(1, m):
        pl.semaphore_signal(
            barrier, inc=1, device_id={"ctx": c, "pb": lax.rem(p + j, m), "row": r},
            device_id_type=MESH,
        )
    pl.semaphore_signal(
        barrier, inc=1, device_id={"ctx": c, "pb": p, "row": 1 - r}, device_id_type=MESH
    )
    for copy in cache_copies + span_copies:
        copy.wait()

    def own_tile(i):
        return packed[c * tiles + i, 0:dk, :].T, packed[c * tiles + i, dk:, :]

    def span_tile(i):
        return near[tail_tiles + i, 0:dk, :].T, near[tail_tiles + i, dk:, :]

    keys, values = own_tile(0)
    lead_k[0], lead_v[0] = keys[:STRIDE], values[:STRIDE]
    keys, values = span_tile(0)
    lead_k[1], lead_v[1] = keys[:STRIDE], values[:STRIDE]

    def head_copies(first):
        return [
            remote(lead_k.at[first], heads_k.at[0], head_send.at[0], head_recv.at[0], ctx=before),
            remote(lead_v.at[first], heads_v.at[0], head_send.at[1], head_recv.at[1], ctx=before),
            remote(lead_k.at[1], heads_k.at[1], head_send.at[2], head_recv.at[2], ctx=before),
            remote(lead_v.at[1], heads_v.at[1], head_send.at[3], head_recv.at[3], ctx=before),
        ]

    pl.semaphore_wait(barrier, n + m - 1)

    @pl.when((r == 1) & (c == 0))
    def _():
        for copy in head_copies(1):
            copy.start()

    @pl.when((r == 1) & (c != 0))
    def _():
        for copy in head_copies(0):
            copy.start()

    def tail_copy(source, part):
        return remote(source, near.at[part], tail_send.at[part], tail_recv.at[part], ctx=after)

    def pair_copy(part):
        return remote(near.at[part], near.at[part], pair_send.at[part], pair_recv.at[part], row=1 - r)

    for part in range(tail_tiles):

        @pl.when((p <= part) & (r == part % 2) & (c == n - 1))
        def _():
            tail_copy(packed.at[c * tiles + tiles - tail_tiles + part], part).start()

        @pl.when((p <= part) & (r == part % 2) & (c != n - 1))
        def _():
            tail_copy(near.at[span_tiles + part], part).start()

    def piece_of(owner, index):
        if tiles >= 2 * m:
            step = tiles // (2 * m)
            return packed.at[pl.ds(owner * tiles + index * step, step)]
        parts = 2 * m // tiles
        rows = tile_rows // parts
        return packed.at[owner * tiles + index // parts, pl.ds(lax.rem(index, parts) * rows, rows)]

    def z_copy(k, owner, target):
        spot = piece_of(owner, place)
        return remote(spot, spot, z_send.at[k - 1], z_recv.at[k - 1], ctx=target)

    for k in range(1, n):
        z_copy(k, c, lax.rem(c + n - k, n)).start()

    def p_copy(k, j, from_pb, target):
        spot = piece_of(lax.rem(c + k, n), from_pb * 2 + r)
        at = (k - 1) * (m - 1) + j - 1
        return remote(spot, spot, p_send.at[at], p_recv.at[at], pb=target)

    def s_copy(k, j, row):
        spot = piece_of(lax.rem(c + k, n), lax.rem(p + m - j, m) * 2 + row)
        at = (k - 1) * m + j
        return remote(spot, spot, s_send.at[at], s_recv.at[at], row=1 - r)

    def forward(k):
        z_copy(k, lax.rem(c + k, n), lax.rem(c + k, n)).wait_recv()
        for j in range(1, m):
            p_copy(k, j, p, lax.rem(p + j, m)).start()
        s_copy(k, 0, r).start()

    def share(k):
        for j in range(1, m):
            p_copy(k, j, lax.rem(p + m - j, m), lax.rem(p + m - j, m)).wait_recv()
            s_copy(k, j, r).start()

    @pl.when(r == 0)
    def _():
        keys, values = own_tile(tiles // 2)
        heads_k[0], heads_v[0] = keys[:STRIDE], values[:STRIDE]
        keys, values = span_tile(span_tiles // 2)
        heads_k[1], heads_v[1] = keys[:STRIDE], values[:STRIDE]

    weights_k, weights_v = pool_keys[...], pool_values[...]

    def half_of(tile_at, count):
        pairs = [tile_at(r * count + i) for i in range(count)]
        return (
            jnp.concatenate([pair[0] for pair in pairs], axis=0),
            jnp.concatenate([pair[1] for pair in pairs], axis=0),
        )

    cache_half = half_of(own_tile, tiles // 2)
    span_half = half_of(span_tile, span_tiles // 2)

    @pl.when(r == 1)
    def _():
        for copy in head_copies(0):
            copy.wait()

    comp[c, r, 1] = jnp.zeros(comp.shape[3:], BF16)
    for which, (keys, values), rows in (
        (0, cache_half, slice(0, comp_cache)),
        (1, span_half, slice(comp_cache, None)),
    ):
        pooled = pool_rows(keys, heads_k[which], weights_k)
        comp[c, r, 0, rows, :] = pooled[:, :LANES]
        comp[c, r, 1, rows, 0 : dk - LANES] = pooled[:, LANES:]
        comp[c, r, 2, rows, :] = pool_rows(values, heads_v[which], weights_v)

    def comp_z(k, owner, target):
        spot = comp.at[owner, r]
        return remote(spot, spot, cz_send.at[k - 1], cz_recv.at[k - 1], ctx=target)

    def comp_s(k, owner, row):
        spot = comp.at[owner, row]
        return remote(spot, spot, cs_send.at[k], cs_recv.at[k], row=1 - r)

    for k in range(1, n):
        comp_z(k, c, lax.rem(c + n - k, n)).start()
    comp_s(0, c, r).start()

    q_copy.wait()
    qa[:, dk:] = jnp.zeros((qa.shape[0], 2 * LANES - dk), BF16)
    for h in range(HEADS):
        qa[h * tokens : (h + 1) * tokens, 0:dk] = q_in[:, h * dk : (h + 1) * dk]

    for part in range(tail_tiles):

        @pl.when((p <= part) & (r == part % 2))
        def _():
            tail_copy(near.at[span_tiles + part], part).wait()
            pair_copy(part).start()

    forward(1)

    sigmoid = jax.nn.sigmoid(gate_logits[...].astype(F32).T)
    for g in range(3):
        for h in range(HEADS):
            column = g * HEADS + h
            gates[g, h * tokens : (h + 1) * tokens, :] = jnp.broadcast_to(
                sigmoid[:, column : column + 1], (tokens, LANES)
            )

    first_pos = n * cache_len + c * span_len + place * tokens

    def token_lane(width):
        return (
            lax.broadcasted_iota(jnp.int32, (tokens, width), 0),
            lax.broadcasted_iota(jnp.int32, (tokens, width), 1),
        )

    token, lane = token_lane(bias_win.shape[1])
    token = token + r * tokens
    bias_win[...] = jnp.where((lane <= token + WINDOW) & (lane > token), 0.0, NEG_FILL)
    token, lane = token_lane(bias_comp.shape[1])
    bias_comp[...] = jnp.where(comp_ends[...] <= token + (first_pos + 1), 0.0, NEG_FILL)
    token, lane = token_lane(bias_sel.shape[1])
    slot, offset = lane >> int(math.log2(BLOCK)), lane & (BLOCK - 1)
    seen = (slot < valid[0]) & ((slot > 0) | (offset <= token))
    bias_sel[...] = jnp.where(seen, 0.0, NEG_FILL)

    group_rows = GROUP * tokens

    def softmax_out(scores, bias, values):
        width = scores.shape[1]
        scores = (scores * scale).reshape(GROUP, tokens, width) + bias[None]
        scores = scores.reshape(group_rows, width)
        highest = jnp.max(scores, axis=1, keepdims=True)
        exponent = jnp.exp(scores - highest)
        total = jnp.sum(exponent, axis=1, keepdims=True)
        numerator = jnp.dot(exponent.astype(BF16), values, preferred_element_type=F32)
        return numerator / total

    for k in range(2, n):
        forward(k)

    for part in range(tail_tiles):

        @pl.when((p <= part) & (r != part % 2))
        def _():
            pair_copy(part).wait_recv()

    near_tiles = [near[p + i] for i in range(tail_tiles + 1)]
    near_k = jnp.concatenate([tile[:dk] for tile in near_tiles], axis=1)
    near_v = jnp.concatenate([tile[dk:] for tile in near_tiles], axis=0)
    sel_k[:, 0 : near_k.shape[1]] = near_k
    sel_v[0 : near_v.shape[0], :] = near_v

    @pl.loop(0, HEADS // GROUP)
    def _(g):
        rows = pl.ds(pl.multiple_of(g * group_rows, group_rows), group_rows)
        scores = jnp.dot(
            qa[rows, 0:dk], sel_k[:, 0 : near_k.shape[1]], preferred_element_type=F32
        )
        acc[rows, :] = gates[2, rows, :] * softmax_out(
            scores, bias_win[...], sel_v[0 : near_v.shape[0], :]
        )

    share(1)

    comp_s(0, c, 1 - r).wait_recv()
    for k in range(1, n):
        owner = lax.rem(c + k, n)
        comp_z(k, owner, owner).wait_recv()
        comp_s(k, owner, r).start()
    for k in range(1, n):
        comp_s(k, lax.rem(c + k, n), 1 - r).wait_recv()
    part_rows = comp.shape[3]
    for owner in range(n):
        for row in range(2):
            low = (owner * 2 + row) * part_rows
            comp_k[low : low + part_rows, 0:LANES] = comp[owner, row, 0]
            comp_k[low : low + part_rows, LANES:] = comp[owner, row, 1]
            comp_v[low : low + part_rows, :] = comp[owner, row, 2]

    @pl.loop(0, HEADS // GROUP)
    def _(g):
        rows = pl.ds(pl.multiple_of(g * group_rows, group_rows), group_rows)
        scores = lax.dot_general(
            qa[rows, :], comp_k[...], (((1,), (1,)), ((), ())), preferred_element_type=F32
        )
        acc[rows, :] += gates[0, rows, :] * softmax_out(scores, bias_comp[...], comp_v[...])

    for k in range(2, n):
        share(k)
    for k in range(1, n):
        for j in range(m):
            s_copy(k, j, 1 - r).wait_recv()

    own = near[tail_tiles + p]
    for s in range(0, picks, 2):
        halves = []
        for slot_at in (s, s + 1):
            if slot_at == 0:
                tile, odd = own, r
            else:
                number = chosen[0, slot_at]
                tile, odd = packed[number >> 1], number & 1
            high = jnp.broadcast_to(odd.astype(F32), (1, BLOCK)).astype(BF16)
            low = jnp.broadcast_to((1 - odd).astype(F32), (1, BLOCK)).astype(BF16)
            halves.append(tile[:dk, :BLOCK] * low + tile[:dk, BLOCK:] * high)
            high = jnp.concatenate([high, high], axis=1)
            low = jnp.concatenate([low, low], axis=1)
            sel_v[slot_at * BLOCK : (slot_at + 1) * BLOCK, :] = (
                tile[dk : dk + BLOCK] * low + tile[dk + BLOCK :] * high
            )
        sel_k[:, s * BLOCK : (s + 2) * BLOCK] = jnp.concatenate(halves, axis=1)

    @pl.loop(0, HEADS // GROUP)
    def _(g):
        rows = pl.ds(pl.multiple_of(g * group_rows, group_rows), group_rows)
        scores = jnp.dot(qa[rows, 0:dk], sel_k[...], preferred_element_type=F32)
        mixed = acc[rows, :] + gates[1, rows, :] * softmax_out(scores, bias_sel[...], sel_v[...])
        for i in range(GROUP):
            column = pl.multiple_of((g * GROUP + i) * LANES, LANES)
            out[:, pl.ds(column, LANES)] = mixed[i * tokens : (i + 1) * tokens].astype(BF16)

    for part in range(tail_tiles):

        @pl.when((p <= part) & (r == part % 2))
        def _():
            pair_copy(part).wait_send()

    for k in range(1, n):
        z_copy(k, c, lax.rem(c + n - k, n)).wait_send()
        comp_z(k, c, lax.rem(c + n - k, n)).wait_send()
        for j in range(1, m):
            p_copy(k, j, p, lax.rem(p + j, m)).wait_send()
        for j in range(m):
            s_copy(k, j, r).wait_send()
    for k in range(n):
        comp_s(k, lax.rem(c + k, n), r).wait_send()


def local(
    queries,
    cache_keys,
    cache_values,
    span_keys,
    span_values,
    pool_keys,
    pool_values,
    gate_logits,
    chosen_blocks,
    valid_counts,
):
    n, m = lax.axis_size("ctx"), lax.axis_size("pb")
    tokens = queries.shape[0]
    cache_len, dk = cache_keys.shape
    dv = cache_values.shape[1]
    span_len = span_keys.shape[0]
    rows = tokens * HEADS
    picks = chosen_blocks.shape[1]
    comp_cache, comp_span = cache_len // 2 // STRIDE, span_len // 2 // STRIDE
    part_rows = comp_cache + comp_span
    shares = np.arange(n * 2)[:, None]
    ids = np.concatenate(
        [
            shares * comp_cache + np.arange(comp_cache)[None],
            2 * n * comp_cache + shares * comp_span + np.arange(comp_span)[None],
        ],
        axis=1,
    ).reshape(1, -1)
    comp_ends = jnp.asarray(ids * STRIDE + CLEN, dtype=jnp.int32)
    tiles, span_tiles, tail_tiles = cache_len // LANES, span_len // LANES, WINDOW // LANES
    sem = pltpu.SemaphoreType.DMA
    anywhere = pl.BlockSpec(memory_space=pl.ANY)
    vmem = pl.BlockSpec(memory_space=pltpu.VMEM)
    smem = pl.BlockSpec(memory_space=pltpu.SMEM)
    keys = n * 2 * part_rows + picks * BLOCK + WINDOW + tokens
    return pl.pallas_call(
        functools.partial(kernel, n, m),
        out_shape=jax.ShapeDtypeStruct((tokens, HEADS * dv), BF16),
        in_specs=[anywhere] * 5 + [vmem] * 4 + [smem] * 2,
        out_specs=vmem,
        scratch_shapes=[
            pltpu.VMEM((tokens, HEADS * dk), BF16),
            pltpu.VMEM((n * tiles, dk + LANES, LANES), BF16),
            pltpu.VMEM((tail_tiles + span_tiles, dk + LANES, LANES), BF16),
            pltpu.VMEM((n, 2, 3, part_rows, LANES), BF16),
            pltpu.VMEM((n * 2 * part_rows, 2 * LANES), BF16),
            pltpu.VMEM((n * 2 * part_rows, dv), BF16),
            pltpu.VMEM((2, STRIDE, dk), BF16),
            pltpu.VMEM((2, STRIDE, dv), BF16),
            pltpu.VMEM((2, STRIDE, dk), BF16),
            pltpu.VMEM((2, STRIDE, dv), BF16),
            pltpu.VMEM((rows, 2 * LANES), BF16),
            pltpu.VMEM((dk, picks * BLOCK), BF16),
            pltpu.VMEM((picks * BLOCK, dv), BF16),
            pltpu.VMEM((3, rows, LANES), F32),
            pltpu.VMEM((rows, dv), F32),
            pltpu.VMEM((tokens, n * 2 * part_rows), F32),
            pltpu.VMEM((tokens, picks * BLOCK), F32),
            pltpu.VMEM((tokens, (tail_tiles + 1) * LANES), F32),
            sem((1,)),
            sem((tiles, 2)),
            sem((span_tiles, 2)),
            sem((4,)),
            sem((4,)),
            sem((tail_tiles,)),
            sem((tail_tiles,)),
            sem((tail_tiles,)),
            sem((tail_tiles,)),
            sem((n - 1,)),
            sem((n - 1,)),
            sem(((n - 1) * (m - 1),)),
            sem(((n - 1) * (m - 1),)),
            sem(((n - 1) * m,)),
            sem(((n - 1) * m,)),
            sem((n - 1,)),
            sem((n - 1,)),
            sem((n,)),
            sem((n,)),
        ],
        compiler_params=pltpu.CompilerParams(
            collective_id=0, has_side_effects=True, vmem_limit_bytes=60 * 1024 * 1024
        ),
        cost_estimate=pl.CostEstimate(
            flops=2 * rows * keys * (dk + dv),
            bytes_accessed=4 * 1024 * 1024,
            transcendentals=rows * keys,
        ),
    )(
        queries,
        cache_keys.T,
        cache_values,
        span_keys.T,
        span_values,
        pool_keys,
        pool_values,
        gate_logits.T,
        comp_ends,
        chosen_blocks,
        valid_counts,
    )


def solution(mesh):
    spread = P(("parts", "ctx", "pb", "row"), None)
    shard = P(("parts", "ctx"), None)
    return jax.shard_map(
        local,
        mesh=mesh,
        in_specs=(
            spread,
            shard,
            shard,
            shard,
            shard,
            P(),
            P(),
            spread,
            spread,
            P(("parts", "ctx", "pb", "row")),
        ),
        out_specs=spread,
        check_vma=False,
    )
```

time: 36.4 us -> 31.8 us (0.87)
  the two profiles are of different devices: /device:TPU:0 before, /device:TPU:1 now
where the time goes in v2:
time: 31.8 us; the launch traced here: 31.6 us
  Pallas kernels  29.2 us (92%)
  local copies, waits for them, and re-layouts  1.67 us (5%)
  between operations  0.66 us (2%)
    pallas_call x1, Pallas kernels, local(): pl.pallas_call(functools.partial(kernel, n, m), out_shape=jax.ShapeDtypeS...  29.2 us
    unnamed x1, local copies, waits for them, and re-layouts  1.67 us

profile of v2, /device:TPU:1, one launch (start us, length us, event | category | flops | bytes accessed | tf_op | source)
XLA Modules:
  0.0 31.6 jit_solution(5254028656986640846)
XLA Ops:
  0.7 29.2 %shard_map.109 = bf16[64,2048]{1,0:T(8,128)(2,1)} custom-call(bf16[64,3072]{1,0:T(8,128)(2,1)} %queries.1, bf16[192,1024]{1,0:T(8,128)(2,1)} %bitcast.3, bf16[1024,128]{1,0:T(8,128)(2,1)} %cache_values.1, bf16[192,512]{1,0:T(8,128)(2,1)} %bitcast.4, bf16[512,128]{1,0:T(8,128)(2,1)} %span_values.1, f32[32,192]{1,0:T(8,128)} %pool_keys.1, ...), custom_call_target="tpu_custom_call" | custom-call | flops 1132462080 | bytes 4194304 | tf_op jit(solution)/shard_map/pallas_call | solution.py:463
  29.9 1.7 %copy.14 = bf16[64,2048]{1,0:T(8,128)(2,1)} copy(bf16[64,2048]{1,0:T(8,128)(2,1)} %shard_map.109) | data formatting | bytes 524288
